TPU v7x, 256 devices: a whole 4x4x8 slice. The times are simulated.
256 devices in a mesh: row: 8 (over x, core), col: 32 (over y, z).
Axes of the slice: x: 4, y: 4, z: 8, core: 2. Of those that a mesh axis runs over, the one named last changes fastest.
Arguments:
- features: bfloat16 [65536, 256], P(('row', 'col')), may hold values from -6 to 6
- neighbours: int32 [10, 65536], P(None, ('row', 'col')), may hold values from 0 to 511, as said below
- halo_ids: int32 [256, 1, 256], P(('row', 'col')), may hold values from 0 to 255
- w_self: bfloat16 [256, 256], replicated, may hold values from -0.375 to 0.375
- w_neigh: bfloat16 [256, 256], replicated, may hold values from -0.75 to 0.75
- b_sage: float32 [256], replicated, may hold values from -3 to 3
- w_first: bfloat16 [512, 256], replicated, may hold values from -0.25 to 0.25
- b_first: float32 [256], replicated, may hold values from -3 to 3
- w_second: bfloat16 [256], replicated, may hold values from -1.5 to 1.5
- b_second: float32 [1], replicated, may hold values from -3 to 3
- src_owner: int32 [8, 32, 8192, 1], P('row', 'col'), may hold values from 0 to 31; in each aligned block of 8192 rows (0 to 8191, 8192 to 16383, ..., all dimensions but the last counted through in order) at most 320 rows name the same one
- src_local: int32 [8, 32, 8192], P('row', 'col'), may hold values from 0 to 255
- dst_index: int32 [8, 32, 8192], P('row', 'col'), may hold values from 0 to 2047
- labels: int32 [8, 32, 8192], P('row', 'col'), may hold values 0 or 1
Outputs:
- embeds: bfloat16 [65536, 256], P(('row', 'col'))
- logits: float32 [8, 32, 8192], P('row', 'col')
- node_grad: float32 [65536, 256], P(('row', 'col'))
- grad_self: float32 [256, 256], replicated
- grad_neigh: float32 [256, 256], replicated
- grad_bsage: float32 [256], replicated
- grad_first: float32 [32, 512, 256], P('col')
- grad_bfirst: float32 [32, 256], P('col')
- grad_second: float32 [32, 256], P('col')
Inputs may be any that keep to these rules, and one draw needn't show every extreme that they name: `neighbours`: in each partition every one of the 256 received rows (values 256 and up) is named by exactly one entry; the other entries name the partition's own rows. `src_owner`: among the 8192 edges of one tile at most 320 name the same source partition, and that many are reached.
All inputs are finite; a program needn't handle non-finite values. No bound on the sum of `labels` on one device may be relied on, other than what follows from the above.
Results may differ from a plain program's by a relative error of at most 0.0052.
Values may be sent and summed in bfloat16 or wider, within the bound.
No kernel may reach another device: no remote copies, remote signals or barrier semaphores. Data moves between devices by JAX's collectives and lax.ppermute only.
A program may use at most 128 MiB of HBM per device.

v0:
```python
import jax
import jax.numpy as jnp
from jax import lax
from jax.sharding import PartitionSpec as P


def per_device(
    features,
    neighbours,
    halo_ids,
    w_self,
    w_neigh,
    b_sage,
    w_first,
    b_first,
    w_second,
    b_second,
    src_owner,
    src_local,
    dst_index,
    labels,
):
    node_dev, feat_width = features.shape
    fanout = neighbours.shape[0]
    row_count = lax.axis_size("row")
    col_count = lax.axis_size("col")
    outgoing = features[halo_ids[0]]
    halo_count = outgoing.shape[0]
    outgoing = outgoing.reshape(halo_count, row_count, col_count, feat_width)
    received = lax.all_to_all(
        lax.all_to_all(outgoing, "row", split_axis=1, concat_axis=1, tiled=True),
        "col",
        split_axis=2,
        concat_axis=2,
        tiled=True,
    )
    extended = jnp.concatenate([features, received.reshape(-1, feat_width)], axis=0)
    gathered = extended[neighbours].astype(jnp.float32)
    aggregate = (jnp.sum(gathered, axis=0) / fanout).astype(jnp.bfloat16)
    embed_f = jnp.dot(features, w_self, preferred_element_type=jnp.float32)
    embed_f = embed_f + jnp.dot(aggregate, w_neigh, preferred_element_type=jnp.float32) + b_sage
    embeds = embed_f.astype(jnp.bfloat16)
    owners = src_owner[0, 0, :, 0]
    local_rows = src_local[0, 0]
    dest_rows = dst_index[0, 0]
    targets = labels[0, 0].astype(jnp.float32)
    edge_count = owners.shape[0]
    src_block = lax.all_gather(embeds, "col", axis=0, tiled=True)
    block_rows = owners * node_dev + local_rows
    src_embed = src_block[block_rows]
    dst_block = lax.all_gather(embeds, "row", axis=0, tiled=True)
    dst_embed = dst_block[dest_rows]
    w_src = w_first[:feat_width]
    w_dst = w_first[feat_width:]
    preact = jnp.dot(src_embed, w_src, preferred_element_type=jnp.float32)
    preact = preact + jnp.dot(dst_embed, w_dst, preferred_element_type=jnp.float32) + b_first
    gate_sig = jax.nn.sigmoid(preact)
    hidden = preact * gate_sig
    hidden_b = hidden.astype(jnp.bfloat16)
    logits = jnp.dot(hidden_b, w_second, preferred_element_type=jnp.float32) + b_second[0]
    dlogit = jax.nn.sigmoid(logits) - targets
    second_f = w_second.astype(jnp.float32)
    dpreact = dlogit[:, None] * second_f[None, :] * gate_sig * (1.0 + preact * (1.0 - gate_sig))
    dpreact_b = dpreact.astype(jnp.bfloat16)
    part_second = jnp.sum(hidden * dlogit[:, None], axis=0)
    part_bfirst = jnp.sum(dpreact, axis=0)
    grad_src = jnp.dot(src_embed.T, dpreact_b, preferred_element_type=jnp.float32)
    grad_dst = jnp.dot(dst_embed.T, dpreact_b, preferred_element_type=jnp.float32)
    part_first = jnp.concatenate([grad_src, grad_dst], axis=0)
    decoder_sums = lax.psum((part_first, part_bfirst, part_second), "row")
    src_rows_g = jnp.dot(dpreact_b, w_src.T, preferred_element_type=jnp.float32).astype(
        jnp.bfloat16
    )
    dst_rows_g = jnp.dot(dpreact_b, w_dst.T, preferred_element_type=jnp.float32).astype(
        jnp.bfloat16
    )
    src_acc = (
        jnp.zeros((src_block.shape[0], feat_width), jnp.float32)
        .at[block_rows]
        .add(src_rows_g.astype(jnp.float32))
    )
    src_grad = lax.psum_scatter(src_acc, "col", scatter_dimension=0, tiled=True)
    dest_acc = (
        jnp.zeros((dst_block.shape[0], feat_width), jnp.float32)
        .at[dest_rows]
        .add(dst_rows_g.astype(jnp.float32))
    )
    dest_grad = lax.psum_scatter(dest_acc, "row", scatter_dimension=0, tiled=True)
    node_grad = src_grad + dest_grad
    node_grad_b = node_grad.astype(jnp.bfloat16)
    part_self = jnp.dot(features.T, node_grad_b, preferred_element_type=jnp.float32)
    part_neigh = jnp.dot(aggregate.T, node_grad_b, preferred_element_type=jnp.float32)
    part_bsage = jnp.sum(node_grad, axis=0)
    encoder_sums = lax.psum((part_self, part_neigh, part_bsage), ("row", "col"))
    return (
        embeds,
        logits.reshape(1, 1, edge_count),
        node_grad,
        encoder_sums[0],
        encoder_sums[1],
        encoder_sums[2],
        decoder_sums[0][None],
        decoder_sums[1][None],
        decoder_sums[2][None],
    )


def solution(mesh):
    placed = (
        P(("row", "col"), None),
        P(None, ("row", "col")),
        P(("row", "col"), None, None),
        P(),
        P(),
        P(),
        P(),
        P(),
        P(),
        P(),
        P("row", "col", None, None),
        P("row", "col", None),
        P("row", "col", None),
        P("row", "col", None),
    )
    return jax.shard_map(
        per_device,
        mesh=mesh,
        in_specs=placed,
        out_specs=(
            P(("row", "col"), None),
            P("row", "col", None),
            P(("row", "col"), None),
            P(),
            P(),
            P(),
            P("col", None, None),
            P("col", None),
            P("col", None),
        ),
        check_vma=False,
    )
```

profile of v0, /device:TPU:8, one launch (start us, length us, event | category | flops | bytes accessed | tf_op | source)
XLA Modules:
  0.0 875.0 jit_solution(14454785513505962907)
XLA Ops:
  7.2 0.7 compare_select_fusion.3
  8.0 2.5 gather_fusion
  10.5 4.4 all-to-all-start
  15.0 0.7 compare_select_fusion.2
  15.7 5.4 all-to-all-done
  21.1 0.7 copy.26
  21.8 11.7 %all-to-all-start.1 = ((bf16[1,8,32,256]{3,1,0,2:T(8,128)(2,1)}), bf16[1,8,32,256]{3,1,0,2:T(8,128)(2,1)S(1)}, u32[]{:S(2)}, u32[]{:S(2)}) async-start(bf16[1,8,32,256]{3,1,0,2:T(8,128)(2,1)} %copy.26), calls=%async_computation.1 | async-start | bytes 262144 | tf_op jit(solution)/shard_map/all_to_all | solution.py:30
  33.6 0.0 all-gather.5.cloned.1.call-start
  33.6 1.1 fusion.26
  34.7 7.9 all-to-all-done.1
  42.7 0.9 pad_maximum_fusion
  43.6 7.6 gather_fusion.1
  51.2 0.2 convert_reduce_fusion
  51.4 0.9 fusion.10
  52.3 0.7 all-gather.3.cloned.1.call-update
  53.0 0.2 reduce-scatter.5.cloned.1.call-start
  54.0 0.1 compare_select_fusion.1
  54.1 18.4 %all-gather.5.cloned.1.call-done = bf16[2048,256]{1,0:T(8,128)(2,1)} async-done(((bf16[256,256]{1,0:T(8,128)(2,1)}), bf16[2048,256]{1,0:T(8,128)(2,1)}) %all-gather.5.cloned.1.call-update) | async-done | bytes 1048592 | tf_op jit(solution)/shard_map/all_gather | solution.py:51
  72.6 32.2 %gather_fusion.3 = bf16[8192,256]{1,0:T(8,128)(2,1)} fusion(bf16[2048,256]{1,0:T(8,128)(2,1)} %all-gather.5.cloned.1.call-done, s32[8192]{0:T(1024)S(1)} %broadcast_clamp_fusion), kind=kCustom, calls=%fused_computation.3 | custom fusion | bytes 8421376 | tf_op jit(solution)/shard_map/gather | solution.py:52
  104.8 51.4 %all-gather.3.cloned.1.call-done = bf16[8192,256]{1,0:T(8,128)(2,1)} async-done(((bf16[256,256]{1,0:T(8,128)(2,1)}), bf16[8192,256]{1,0:T(8,128)(2,1)}) %all-gather.3.cloned.1.call-update) | async-done | bytes 4194320 | tf_op jit(solution)/shard_map/all_gather | solution.py:48
  156.2 33.6 %gather_fusion.2 = bf16[8192,256]{1,0:T(8,128)(2,1)} fusion(bf16[8192,256]{1,0:T(8,128)(2,1)} %all-gather.3.cloned.1.call-done, s32[8192]{0:T(1024)S(1)} %broadcast_clamp_fusion.1), kind=kCustom, calls=%fused_computation.2 | custom fusion | bytes 8421376 | tf_op jit(solution)/shard_map/gather | solution.py:50
  189.8 3.6 fusion.16
  193.4 1.3 fusion
  194.7 2.4 fusion.6
  197.1 0.6 divide_subtract_fusion
  197.8 5.9 fusion.24
  203.6 2.0 copy-done.2
  205.6 4.5 fusion.1
  210.1 46.0 %scatter_custom_fusion.1 = f32[2048,256]{1,0:T(8,128)} fusion(s32[8192]{0:T(1024)S(1)} %bitcast.48, f32[8192,256]{1,0:T(8,128)} %fusion.1, f32[]{:T(128)} %constant.11.clone.1), kind=kCustom, calls=%fused_computation.25 | custom fusion | flops 2097152 | bytes 2097664 | tf_op jit(solution)/shard_map/scatter-add | solution.py:86
  256.2 0.3 reduce-scatter.3.cloned.1.call-start
  256.4 6.7 fusion.2
  263.1 48.3 %scatter_custom_fusion = f32[8192,256]{1,0:T(8,128)} fusion(s32[8192]{0:T(1024)S(1)} %bitcast.46, f32[8192,256]{1,0:T(8,128)} %fusion.2, f32[]{:T(128)} %constant.11.clone.1), kind=kCustom, calls=%fused_computation.16 | custom fusion | flops 2097152 | bytes 8389120 | tf_op jit(solution)/shard_map/scatter-add | solution.py:80
  311.5 0.0 all-reduce.7.cloned.1.call-start
  311.5 4.8 fusion.27
  316.3 221.9 %reduce-scatter.3.cloned.1.call-done = f32[256,256]{1,0:T(8,128)} async-done(((f32[8192,256]{1,0:T(8,128)}), f32[256,256]{1,0:T(8,128)}) %reduce-scatter.3.cloned.1.call-update) | async-done | bytes 262160 | tf_op jit(solution)/shard_map/reduce_scatter | solution.py:82
  538.3 1.1 fusion.25
  539.4 0.9 fusion.18
  540.3 0.9 convolution_bitcast_fusion
  541.3 0.0 all-reduce.5.cloned.1.call-start
  541.3 4.8 fusion.28
  546.1 0.8 maximum_bitcast_fusion
  547.0 13.0 %all-reduce.1 = (f32[1,256]{1,0:T(1,128)}, f32[1,256]{1,0:T(1,128)}) all-reduce(f32[1,256]{1,0:T(1,128)S(1)} %bitcast.52, f32[1,256]{1,0:T(1,128)S(1)} %bitcast.53), channel_id=1, replica_groups=mesh['row'=8,'col'=32] {'row'}, use_global_device_ids=true, to_apply=%region_11.0 | all-reduce | flops 512 | bytes 4096 | tf_op jit(solution)/shard_map/psum | solution.py:70
  560.0 74.7 %psum.44 = f32[256]{0:T(256)} all-reduce(f32[256]{0:T(256)S(1)} %get-tuple-element.42), channel_id=1, replica_groups=mesh['row'=8,'col'=32] {'row','col'}, use_global_device_ids=true, to_apply=%region_8.0 | all-reduce | flops 256 | bytes 2048 | tf_op jit(solution)/shard_map/psum | solution.py:94
  634.6 162.6 %all-reduce.7.cloned.1.call-done = (f32[256,256]{0,1:T(8,128)}, f32[256,256]{1,0:T(8,128)}) async-done(((f32[256,256]{0,1:T(8,128)}, f32[256,256]{1,0:T(8,128)}), (f32[256,256]{0,1:T(8,128)}, f32[256,256]{1,0:T(8,128)})) %all-reduce.7.cloned.1.call-update) | async-done | bytes 524304 | tf_op jit(solution)/shard_map/psum | solution.py:94
  797.2 1.8 copy.28
  799.0 65.6 %all-reduce.5.cloned.1.call-done = f32[1,512,256]{2,1,0:T(8,128)} async-done(((f32[1,512,256]{2,1,0:T(8,128)}), f32[1,512,256]{2,1,0:T(8,128)}) %all-reduce.5.cloned.1.call-update) | async-done | bytes 524304 | tf_op jit(solution)/shard_map/psum | solution.py:70
  864.6 1.7 copy.33
  866.2 1.9 copy.34
  (46 shorter events, 0.3 us)
Async XLA Ops:
  7.2 26.4 %copy-start = (bf16[256,256]{1,0:T(8,128)(2,1)S(1)}, bf16[256,256]{1,0:T(8,128)(2,1)}, u32[]{:S(2)}) copy-start(bf16[256,256]{1,0:T(8,128)(2,1)} %param.17) | copy-start | bytes 393220
  7.2 44.2 %copy-start.13 = (f32[256]{0:T(256)S(1)}, f32[256]{0:T(256)}, u32[]{:S(2)}) copy-start(f32[256]{0:T(256)} %param.19) | copy-start | bytes 3076
  7.2 44.2 %copy-start.7 = (bf16[256,256]{1,0:T(8,128)(2,1)S(1)}, bf16[256,256]{1,0:T(8,128)(2,1)}, u32[]{:S(2)}) copy-start(bf16[256,256]{1,0:T(8,128)(2,1)} %param.18) | copy-start | bytes 393220
  10.5 42.7 %copy-start.14 = (bf16[256]{0:T(256)(128)(2,1)S(1)}, bf16[256]{0:T(256)(128)(2,1)}, u32[]{:S(2)}) copy-start(bf16[256]{0:T(256)(128)(2,1)} %param.22) | copy-start | bytes 1540
  10.5 43.4 %copy-start.10 = (s32[1,1,8192]{2,1,0:T(1,128)S(1)}, s32[1,1,8192]{2,1,0:T(1,128)}, u32[]{:S(2)}) copy-start(s32[1,1,8192]{2,1,0:T(1,128)} %param.27) | copy-start | bytes 98308
  10.5 43.4 %copy-start.8 = (s32[1,1,8192]{2,1,0:T(1,128)S(1)}, s32[1,1,8192]{2,1,0:T(1,128)}, u32[]{:S(2)}) copy-start(s32[1,1,8192]{2,1,0:T(1,128)} %param.25) | copy-start | bytes 98308
  10.5 43.5 %copy-start.9 = (s32[1,1,8192,1]{2,3,1,0:T(1,128)S(1)}, s32[1,1,8192,1]{2,3,1,0:T(1,128)}, u32[]{:S(2)}) copy-start(s32[1,1,8192,1]{2,3,1,0:T(1,128)} %param.24) | copy-start | bytes 98308
  10.5 43.5 %copy-start.11 = (s32[1,1,8192]{2,1,0:T(1,128)S(1)}, s32[1,1,8192]{2,1,0:T(1,128)}, u32[]{:S(2)}) copy-start(s32[1,1,8192]{2,1,0:T(1,128)} %param.26) | copy-start | bytes 98308
  10.5 10.6 %all-to-all-start = ((bf16[1,8,32,256]{3,2,0,1:T(8,128)(2,1)}), bf16[1,8,32,256]{3,2,0,1:T(8,128)(2,1)S(1)}, u32[]{:S(2)}, u32[]{:S(2)}) async-start(bf16[1,8,32,256]{3,2,0,1:T(8,128)(2,1)} %bitcast.3), calls=%async_computation | async-start | bytes 262144 | tf_op jit(solution)/shard_map/all_to_all | solution.py:31
  21.8 20.8 %all-to-all-start.1 = ((bf16[1,8,32,256]{3,1,0,2:T(8,128)(2,1)}), bf16[1,8,32,256]{3,1,0,2:T(8,128)(2,1)S(1)}, u32[]{:S(2)}, u32[]{:S(2)}) async-start(bf16[1,8,32,256]{3,1,0,2:T(8,128)(2,1)} %copy.26), calls=%async_computation.1 | async-start | bytes 262144 | tf_op jit(solution)/shard_map/all_to_all | solution.py:30
  33.6 39.0 %all-gather.5.cloned.1.call-start = ((), (), s32[]{:S(2)}) async-start(), calls=%async_computation.5 | async-start | bytes 1179648 | tf_op jit(solution)/shard_map/all_gather | solution.py:51
  52.3 103.9 %all-gather.3.cloned.1.call-start = ((), (), s32[]{:S(2)}) async-start(), calls=%async_computation.4 | async-start | bytes 4325376 | tf_op jit(solution)/shard_map/all_gather | solution.py:48
  53.0 263.3 %reduce-scatter.5.cloned.1.call-start = ((), (), s32[]{:S(2)}) async-start(), calls=%async_computation.7 | async-start | bytes 2359296 | tf_op jit(solution)/shard_map/reduce_scatter | solution.py:88
  104.8 85.0 %copy-start.6 = (bf16[512,256]{1,0:T(8,128)(2,1)S(1)}, bf16[512,256]{1,0:T(8,128)(2,1)}, u32[]{:S(2)}) copy-start(bf16[512,256]{1,0:T(8,128)(2,1)} %param.20) | copy-start | bytes 786436
  189.8 3.6 copy-start.3
  189.8 3.6 copy-start.12
  203.6 2.0 copy-start.2
  256.2 282.1 %reduce-scatter.3.cloned.1.call-start = ((), (), s32[]{:S(2)}) async-start(), calls=%async_computation.6 | async-start | bytes 8650752 | tf_op jit(solution)/shard_map/reduce_scatter | solution.py:82
  311.5 228.8 %copy-start.4 = (bf16[256,256]{1,0:T(8,128)(2,1)S(1)}, bf16[256,256]{1,0:T(8,128)(2,1)}, u32[]{:S(2)}) copy-start(bf16[256,256]{1,0:T(8,128)(2,1)} %param.14) | copy-start | bytes 393220
  311.5 485.7 %all-reduce.7.cloned.1.call-start = ((), (), s32[]{:S(2)}) async-start(), calls=%async_computation.9 | async-start | bytes 1048576 | tf_op jit(solution)/shard_map/psum | solution.py:94
  539.4 6.7 copy-start.5
  541.3 326.8 %copy-start.1 = (bf16[256,256]{1,0:T(8,128)(2,1)S(1)}, bf16[256,256]{1,0:T(8,128)(2,1)}, u32[]{:S(2)}) copy-start(bf16[256,256]{1,0:T(8,128)(2,1)} %param.17) | copy-start | bytes 393220
  541.3 323.3 %all-reduce.5.cloned.1.call-start = ((), (), s32[]{:S(2)}) async-start(), calls=%async_computation.8 | async-start | bytes 1048576 | tf_op jit(solution)/shard_map/psum | solution.py:70
Sparse Core Ops, SparseCore 0:
  52.4 20.1 all-gather.4
  75.7 80.4 all-gather.2
  256.3 34.6 reduce-scatter.4
  311.6 226.6 reduce-scatter.2
  545.3 251.9 all-reduce.6
  800.1 64.4 all-reduce.4
where the time goes:
time: 876 us; the launch traced here: 875 us
  waiting for transfers between devices  534 us (61%)
  other arithmetic  105 us (12%)
  blocking collectives  87.7 us (10%)
  local copies, waits for them, and re-layouts  84.1 us (10%)
  matrix products  31.8 us (4%)
  starting transfers between devices  16.8 us (2%)
  between operations  15.1 us (2%)
    reduce_scatter x1, waiting for transfers between devices, per_device(): src_grad = lax.psum_scatter(src_acc, 'col', scatter_dimension=0, tiled=True)  222 us
    psum x1, waiting for transfers between devices, per_device(): encoder_sums = lax.psum((part_self, part_neigh, part_bsage), ('row', 'col'))  163 us
    psum x1, blocking collectives, per_device(): encoder_sums = lax.psum((part_self, part_neigh, part_bsage), ('row', 'col'))  74.7 us
    psum x1, waiting for transfers between devices, per_device(): decoder_sums = lax.psum((part_first, part_bfirst, part_second), 'row')  65.6 us
    all_gather x1, waiting for transfers between devices, per_device(): src_block = lax.all_gather(embeds, 'col', axis=0, tiled=True)  51.4 us
    scatter-add x1, other arithmetic, per_device(): src_acc = jnp.zeros((src_block.shape[0], feat_width), jnp.float32).at[blo...  48.3 us
    scatter-add x1, other arithmetic, per_device(): dest_acc = jnp.zeros((dst_block.shape[0], feat_width), jnp.float32).at[de...  46 us
    gather x1, local copies, waits for them, and re-layouts, per_device(): src_embed = src_block[block_rows]  33.6 us
  transfers between devices with their start and end apart: 8, of which 7 were waited for; matrix products, arithmetic and copies ran while one was open for 12% of the time, Pallas kernels for 0%

commit v1 on v0

--- a/solution.py
+++ b/solution.py
@@ -48,7 +48,9 @@
     src_block = lax.all_gather(embeds, "col", axis=0, tiled=True)
     block_rows = owners * node_dev + local_rows
     src_embed = src_block[block_rows]
-    dst_block = lax.all_gather(embeds, "row", axis=0, tiled=True)
+    dst_block = jnp.concatenate(
+        lax.all_to_all(jnp.stack([embeds] * lax.axis_size("row")), "row", 0, 0), axis=0
+    )
     dst_embed = dst_block[dest_rows]
     w_src = w_first[:feat_width]
     w_dst = w_first[feat_width:]

time: 876 us -> 847 us (0.967)
  waiting for transfers between devices: 534 us -> 499 us
    all_gather x1, waiting for transfers between devices: 51.4 us -> 20.4 us  [per_device(): src_block = lax.all_gather(embeds, 'col', axis=0, tiled=True)]
    all_gather x1 -> x0, waiting for transfers between devices: 18.4 us -> none  [per_device(): dst_block = lax.all_gather(embeds, 'row', axis=0, tiled=True)]
    all_to_all x0 -> x1, waiting for transfers between devices: none -> 14.8 us  [per_device(): lax.all_to_all(jnp.stack([embeds] * lax.axis_size('row')), 'row', 0, 0)]
where the time goes in v1:
time: 847 us; the launch traced here: 846 us
  waiting for transfers between devices  499 us (59%)
  other arithmetic  105 us (12%)
  blocking collectives  87.4 us (10%)
  local copies, waits for them, and re-layouts  87 us (10%)
  matrix products  31.8 us (4%)
  starting transfers between devices  20.3 us (2%)
  between operations  14.8 us (2%)
    reduce_scatter x1, waiting for transfers between devices, per_device(): src_grad = lax.psum_scatter(src_acc, 'col', scatter_dimension=0, tiled=True)  222 us
    psum x1, waiting for transfers between devices, per_device(): encoder_sums = lax.psum((part_self, part_neigh, part_bsage), ('row', 'col'))  163 us
    psum x1, blocking collectives, per_device(): encoder_sums = lax.psum((part_self, part_neigh, part_bsage), ('row', 'col'))  74.4 us
    psum x1, waiting for transfers between devices, per_device(): decoder_sums = lax.psum((part_first, part_bfirst, part_second), 'row')  65.6 us
    scatter-add x1, other arithmetic, per_device(): src_acc = jnp.zeros((src_block.shape[0], feat_width), jnp.float32).at[blo...  48.3 us
    scatter-add x1, other arithmetic, per_device(): dest_acc = jnp.zeros((dst_block.shape[0], feat_width), jnp.float32).at[de...  46 us
    gather x1, local copies, waits for them, and re-layouts, per_device(): src_embed = src_block[block_rows]  33.8 us
    gather x1, local copies, waits for them, and re-layouts, per_device(): dst_embed = dst_block[dest_rows]  33.1 us
  transfers between devices with their start and end apart: 8, of which 7 were waited for; matrix products, arithmetic and copies ran while one was open for 12% of the time, Pallas kernels for 0%

profile of v1, /device:TPU:8, one launch (start us, length us, event | category | flops | bytes accessed | tf_op | source)
XLA Modules:
  0.0 845.8 jit_solution(1929848106204975336)
XLA Ops:
  7.2 0.7 compare_select_fusion.3
  8.0 2.5 gather_fusion
  10.5 4.4 all-to-all-start
  14.9 0.7 compare_select_fusion.2
  15.7 5.4 all-to-all-done
  21.1 0.7 copy.26
  21.8 11.7 %all-to-all-start.1 = ((bf16[1,8,32,256]{3,1,0,2:T(8,128)(2,1)}), bf16[1,8,32,256]{3,1,0,2:T(8,128)(2,1)S(1)}, u32[]{:S(2)}, u32[]{:S(2)}) async-start(bf16[1,8,32,256]{3,1,0,2:T(8,128)(2,1)} %copy.26), calls=%async_computation.1 | async-start | bytes 262144 | tf_op jit(solution)/shard_map/all_to_all | solution.py:30
  33.6 1.1 fusion.26
  34.7 7.9 all-to-all-done.1
  42.6 0.9 pad_maximum_fusion
  43.6 7.6 gather_fusion.1
  51.2 0.2 convert_reduce_fusion
  51.4 0.9 fusion.10
  52.3 0.1 compare_select_fusion.1
  52.3 1.9 stack.2
  54.3 3.6 all-to-all-start.2
  57.8 0.2 reduce-scatter.5.cloned.1.call-start
  58.9 14.8 %all-to-all-done.2 = bf16[8,256,256]{2,1,0:T(8,128)(2,1)S(1)} async-done(((bf16[8,256,256]{2,1,0:T(8,128)(2,1)}), bf16[8,256,256]{2,1,0:T(8,128)(2,1)S(1)}, u32[]{:S(2)}, u32[]{:S(2)}) %all-to-all-start.2) | async-done | bytes 1048608 | tf_op jit(solution)/shard_map/all_to_all | solution.py:52
  73.7 33.1 %gather_fusion.3 = bf16[8192,256]{1,0:T(8,128)(2,1)} fusion(bf16[2048,256]{1,0:T(8,128)(2,1)S(1)} %bitcast.44, s32[8192]{0:T(1024)S(1)} %broadcast_clamp_fusion), kind=kCustom, calls=%fused_computation.3 | custom fusion | bytes 8421376 | tf_op jit(solution)/shard_map/gather | solution.py:54
  106.8 20.4 %all-gather.2.cloned.1.call-done = bf16[8192,256]{1,0:T(8,128)(2,1)} async-done(((bf16[256,256]{1,0:T(8,128)(2,1)}), bf16[8192,256]{1,0:T(8,128)(2,1)}) %all-gather.2.cloned.1.call-update) | async-done | bytes 4194320 | tf_op jit(solution)/shard_map/all_gather | solution.py:48
  127.2 33.8 %gather_fusion.2 = bf16[8192,256]{1,0:T(8,128)(2,1)} fusion(bf16[8192,256]{1,0:T(8,128)(2,1)} %all-gather.2.cloned.1.call-done, s32[8192]{0:T(1024)S(1)} %broadcast_clamp_fusion.1), kind=kCustom, calls=%fused_computation.2 | custom fusion | bytes 8421376 | tf_op jit(solution)/shard_map/gather | solution.py:50
  161.0 3.6 fusion.16
  164.6 1.3 fusion
  165.9 2.4 fusion.6
  168.3 0.6 divide_subtract_fusion
  168.9 5.9 fusion.24
  174.8 2.0 copy-done.2
  176.8 4.5 fusion.1
  181.3 46.0 %scatter_custom_fusion.1 = f32[2048,256]{1,0:T(8,128)} fusion(s32[8192]{0:T(1024)S(1)} %bitcast.50, f32[8192,256]{1,0:T(8,128)} %fusion.1, f32[]{:T(128)} %constant.11.clone.1), kind=kCustom, calls=%fused_computation.25 | custom fusion | flops 2097152 | bytes 2097664 | tf_op jit(solution)/shard_map/scatter-add | solution.py:88
  227.3 0.3 reduce-scatter.3.cloned.1.call-start
  227.6 6.7 fusion.2
  234.3 48.3 %scatter_custom_fusion = f32[8192,256]{1,0:T(8,128)} fusion(s32[8192]{0:T(1024)S(1)} %bitcast.48, f32[8192,256]{1,0:T(8,128)} %fusion.2, f32[]{:T(128)} %constant.11.clone.1), kind=kCustom, calls=%fused_computation.16 | custom fusion | flops 2097152 | bytes 8389120 | tf_op jit(solution)/shard_map/scatter-add | solution.py:82
  282.6 0.0 all-reduce.7.cloned.1.call-start
  282.7 4.8 fusion.27
  287.5 222.0 %reduce-scatter.3.cloned.1.call-done = f32[256,256]{1,0:T(8,128)} async-done(((f32[8192,256]{1,0:T(8,128)}), f32[256,256]{1,0:T(8,128)}) %reduce-scatter.3.cloned.1.call-update) | async-done | bytes 262160 | tf_op jit(solution)/shard_map/reduce_scatter | solution.py:84
  509.5 1.1 fusion.25
  510.6 0.9 fusion.18
  511.5 0.9 convolution_bitcast_fusion
  512.5 0.0 all-reduce.5.cloned.1.call-start
  512.6 4.8 fusion.28
  517.3 0.8 maximum_bitcast_fusion
  518.2 13.0 %all-reduce.1 = (f32[1,256]{1,0:T(1,128)}, f32[1,256]{1,0:T(1,128)}) all-reduce(f32[1,256]{1,0:T(1,128)S(1)} %bitcast.54, f32[1,256]{1,0:T(1,128)S(1)} %bitcast.55), channel_id=1, replica_groups=mesh['row'=8,'col'=32] {'row'}, use_global_device_ids=true, to_apply=%region_11.0 | all-reduce | flops 512 | bytes 4096 | tf_op jit(solution)/shard_map/psum | solution.py:72
  531.2 74.4 %psum.44 = f32[256]{0:T(256)} all-reduce(f32[256]{0:T(256)S(1)} %get-tuple-element.42), channel_id=1, replica_groups=mesh['row'=8,'col'=32] {'row','col'}, use_global_device_ids=true, to_apply=%region_8.0 | all-reduce | flops 256 | bytes 2048 | tf_op jit(solution)/shard_map/psum | solution.py:96
  605.6 162.8 %all-reduce.7.cloned.1.call-done = (f32[256,256]{0,1:T(8,128)}, f32[256,256]{1,0:T(8,128)}) async-done(((f32[256,256]{0,1:T(8,128)}, f32[256,256]{1,0:T(8,128)}), (f32[256,256]{0,1:T(8,128)}, f32[256,256]{1,0:T(8,128)})) %all-reduce.7.cloned.1.call-update) | async-done | bytes 524304 | tf_op jit(solution)/shard_map/psum | solution.py:96
  768.4 1.8 copy.28
  770.2 65.6 %all-reduce.5.cloned.1.call-done = f32[1,512,256]{2,1,0:T(8,128)} async-done(((f32[1,512,256]{2,1,0:T(8,128)}), f32[1,512,256]{2,1,0:T(8,128)}) %all-reduce.5.cloned.1.call-update) | async-done | bytes 524304 | tf_op jit(solution)/shard_map/psum | solution.py:72
  835.7 1.7 copy.33
  837.4 1.9 copy.34
  (46 shorter events, 0.3 us)
Async XLA Ops:
  7.2 26.4 %copy-start = (bf16[256,256]{1,0:T(8,128)(2,1)S(1)}, bf16[256,256]{1,0:T(8,128)(2,1)}, u32[]{:S(2)}) copy-start(bf16[256,256]{1,0:T(8,128)(2,1)} %param.17) | copy-start | bytes 393220
  7.2 44.2 %copy-start.13 = (f32[256]{0:T(256)S(1)}, f32[256]{0:T(256)}, u32[]{:S(2)}) copy-start(f32[256]{0:T(256)} %param.19) | copy-start | bytes 3076
  7.2 44.2 %copy-start.7 = (bf16[256,256]{1,0:T(8,128)(2,1)S(1)}, bf16[256,256]{1,0:T(8,128)(2,1)}, u32[]{:S(2)}) copy-start(bf16[256,256]{1,0:T(8,128)(2,1)} %param.18) | copy-start | bytes 393220
  10.5 41.8 %copy-start.8 = (s32[1,1,8192]{2,1,0:T(1,128)S(1)}, s32[1,1,8192]{2,1,0:T(1,128)}, u32[]{:S(2)}) copy-start(s32[1,1,8192]{2,1,0:T(1,128)} %param.25) | copy-start | bytes 98308
  10.5 41.8 %copy-start.9 = (s32[1,1,8192,1]{2,3,1,0:T(1,128)S(1)}, s32[1,1,8192,1]{2,3,1,0:T(1,128)}, u32[]{:S(2)}) copy-start(s32[1,1,8192,1]{2,3,1,0:T(1,128)} %param.24) | copy-start | bytes 98308
  10.5 10.6 %all-to-all-start = ((bf16[1,8,32,256]{3,2,0,1:T(8,128)(2,1)}), bf16[1,8,32,256]{3,2,0,1:T(8,128)(2,1)S(1)}, u32[]{:S(2)}, u32[]{:S(2)}) async-start(bf16[1,8,32,256]{3,2,0,1:T(8,128)(2,1)} %bitcast.3), calls=%async_computation | async-start | bytes 262144 | tf_op jit(solution)/shard_map/all_to_all | solution.py:31
  21.8 20.8 %all-to-all-start.1 = ((bf16[1,8,32,256]{3,1,0,2:T(8,128)(2,1)}), bf16[1,8,32,256]{3,1,0,2:T(8,128)(2,1)S(1)}, u32[]{:S(2)}, u32[]{:S(2)}) async-start(bf16[1,8,32,256]{3,1,0,2:T(8,128)(2,1)} %copy.26), calls=%async_computation.1 | async-start | bytes 262144 | tf_op jit(solution)/shard_map/all_to_all | solution.py:30
  33.5 93.7 %all-gather.2.cloned.1.call-start = ((), (), s32[]{:S(2)}) async-start(), calls=%async_computation.5 | async-start | bytes 4325376 | tf_op jit(solution)/shard_map/all_gather | solution.py:48
  43.6 14.5 %copy-start.10 = (s32[1,1,8192]{2,1,0:T(1,128)S(1)}, s32[1,1,8192]{2,1,0:T(1,128)}, u32[]{:S(2)}) copy-start(s32[1,1,8192]{2,1,0:T(1,128)} %param.26) | copy-start | bytes 98308
  43.6 14.6 %copy-start.14 = (bf16[256]{0:T(256)(128)(2,1)S(1)}, bf16[256]{0:T(256)(128)(2,1)}, u32[]{:S(2)}) copy-start(bf16[256]{0:T(256)(128)(2,1)} %param.22) | copy-start | bytes 1540
  43.6 15.2 %copy-start.11 = (s32[1,1,8192]{2,1,0:T(1,128)S(1)}, s32[1,1,8192]{2,1,0:T(1,128)}, u32[]{:S(2)}) copy-start(s32[1,1,8192]{2,1,0:T(1,128)} %param.27) | copy-start | bytes 98308
  54.3 19.4 %all-to-all-start.2 = ((bf16[8,256,256]{2,1,0:T(8,128)(2,1)}), bf16[8,256,256]{2,1,0:T(8,128)(2,1)S(1)}, u32[]{:S(2)}, u32[]{:S(2)}) async-start(bf16[8,256,256]{2,1,0:T(8,128)(2,1)} %stack.2), calls=%async_computation.2 | async-start | bytes 2097152 | tf_op jit(solution)/shard_map/all_to_all | solution.py:52
  57.8 229.6 %reduce-scatter.5.cloned.1.call-start = ((), (), s32[]{:S(2)}) async-start(), calls=%async_computation.7 | async-start | bytes 2359296 | tf_op jit(solution)/shard_map/reduce_scatter | solution.py:90
  106.8 54.2 %copy-start.6 = (bf16[512,256]{1,0:T(8,128)(2,1)S(1)}, bf16[512,256]{1,0:T(8,128)(2,1)}, u32[]{:S(2)}) copy-start(bf16[512,256]{1,0:T(8,128)(2,1)} %param.20) | copy-start | bytes 786436
  161.0 3.6 copy-start.3
  161.0 3.6 copy-start.12
  174.8 2.0 copy-start.2
  227.3 282.2 %reduce-scatter.3.cloned.1.call-start = ((), (), s32[]{:S(2)}) async-start(), calls=%async_computation.6 | async-start | bytes 8650752 | tf_op jit(solution)/shard_map/reduce_scatter | solution.py:84
  282.6 228.9 %copy-start.4 = (bf16[256,256]{1,0:T(8,128)(2,1)S(1)}, bf16[256,256]{1,0:T(8,128)(2,1)}, u32[]{:S(2)}) copy-start(bf16[256,256]{1,0:T(8,128)(2,1)} %param.14) | copy-start | bytes 393220
  282.6 485.8 %all-reduce.7.cloned.1.call-start = ((), (), s32[]{:S(2)}) async-start(), calls=%async_computation.9 | async-start | bytes 1048576 | tf_op jit(solution)/shard_map/psum | solution.py:96
  510.6 6.7 copy-start.5
  512.5 326.8 %copy-start.1 = (bf16[256,256]{1,0:T(8,128)(2,1)S(1)}, bf16[256,256]{1,0:T(8,128)(2,1)}, u32[]{:S(2)}) copy-start(bf16[256,256]{1,0:T(8,128)(2,1)} %param.17) | copy-start | bytes 393220
  512.5 323.2 %all-reduce.5.cloned.1.call-start = ((), (), s32[]{:S(2)}) async-start(), calls=%async_computation.8 | async-start | bytes 1048576 | tf_op jit(solution)/shard_map/psum | solution.py:72
Sparse Core Ops, SparseCore 0:
  52.4 74.7 all-gather.1
  227.4 34.5 reduce-scatter.4
  282.7 226.7 reduce-scatter.2
  516.5 251.8 all-reduce.6
  771.3 64.4 all-reduce.4
